TPU v7x, 256 devices: a whole 4x4x8 slice. The times are simulated.
256 devices in a mesh: fam: 8 (over y_hi, x), owner: 32 (over y_lo, z, core).
Axes of the slice: x: 4, y: 4 (y_hi: 2, y_lo: 2; y = y_hi * 2 + y_lo), z: 8, core: 2. Of those that a mesh axis runs over, the one named last changes fastest.
Arguments:
- wavefunction: bfloat16 [16384, 512], P('owner'), may hold values from -6 to 6
- left_blocks: bfloat16 [8, 8, 16384, 1024], P('fam', None, 'owner'), may hold values from -0.1875 to 0.1875
- right_blocks: bfloat16 [8, 512, 512], P('fam'), may hold values from -0.0625 to 0.0625
- term_sources: int32 [8, 16, 8], replicated, may hold values from 0 to 15
- term_counts: int32 [8, 16], replicated, may hold values from 1 to 8, as said below
- sector_rows: int32 [16], replicated, may hold values from 256 to 1024
Outputs:
- sigma: bfloat16 [16384, 512], P('owner', 'fam')
Inputs may be any that keep to these rules, and one draw needn't show every extreme that they name: `term_counts`: every entry lies in 1 to 8; for every output sector some family has exactly 8 live slots.
All inputs are finite; a program needn't handle non-finite values.
Results may differ from a plain program's by a relative error of at most 0.0095.
Values may be sent and summed in bfloat16 or wider, within the bound.
A program may use at most 128 MiB of HBM per device.

v0:
```python
import jax
import jax.numpy as jnp
from jax import lax
from jax.sharding import PartitionSpec as P


def in_blocks(value, dim, count):
    dims = value.shape
    parts = value.reshape(*dims[:dim], count, dims[dim] // count, *dims[dim + 1 :])
    return jnp.moveaxis(parts, dim, 0)


def sent_and_summed(value, axis, dim):
    count = lax.axis_size(axis)
    parts = lax.all_to_all(in_blocks(value, dim, count), axis, 0, 0, tiled=True)
    return jnp.sum(parts, axis=0)


def row_keep(global_rows, sector_len, sector_rows):
    sector = global_rows // sector_len
    table = jnp.arange(sector_rows.shape[0], dtype=jnp.int32)
    used = jnp.sum(jnp.where(sector[:, None] == table[None, :], sector_rows[None, :], 0), axis=1)
    return global_rows % sector_len < used


def body(wavefunction, left_blocks, right_blocks, term_sources, term_counts, sector_rows):
    rows_dev, columns = wavefunction.shape
    slot_count = left_blocks.shape[1]
    sector_len = left_blocks.shape[3]
    fam_here = lax.axis_index("fam")
    first_row = lax.axis_index("owner") * rows_dev
    global_rows = first_row + jnp.arange(rows_dev, dtype=jnp.int32)
    keep = row_keep(global_rows, sector_len, sector_rows)
    masked = jnp.where(keep[:, None], wavefunction, jnp.zeros_like(wavefunction))
    out_sector = [(first_row + 0) // sector_len]
    slot_ids = jnp.arange(slot_count, dtype=jnp.int32)
    items = left_blocks[0]
    right_stack = right_blocks[0]
    block = 0
    live = [slot_ids < term_counts[fam_here, out_sector[block]]]
    source = term_sources[fam_here, out_sector[block], slot_ids]
    whole = lax.all_gather(masked, "owner", axis=0, tiled=True)
    stacked = whole.reshape(whole.shape[0] // sector_len, sector_len, whole.shape[1])
    sources = jnp.take(stacked, source, axis=0)
    accum = jnp.stack(
        [jnp.einsum("kri,kic->krc", items, sources, preferred_element_type=jnp.float32)], axis=0
    )
    partial_value = accum.astype(jnp.bfloat16)
    block = 0
    used = jnp.where(
        live[block][:, None, None], partial_value[block], jnp.zeros_like(partial_value[block])
    )
    total = jnp.einsum("krc,cd->rd", used, right_stack, preferred_element_type=jnp.float32)
    combined = total
    combined = jnp.where(keep[:, None], combined, jnp.zeros_like(combined))
    summed = sent_and_summed(combined, "fam", 1)
    return summed.astype(jnp.bfloat16)


def solution(mesh):
    return jax.shard_map(
        body,
        mesh=mesh,
        in_specs=(
            P("owner", None),
            P("fam", None, "owner", None),
            P("fam", None, None),
            P(),
            P(),
            P(),
        ),
        out_specs=P("owner", "fam"),
        check_vma=False,
    )
```

profile of v0, /device:TPU:1, one launch (start us, length us, event | category | flops | bytes accessed | tf_op | source)
XLA Modules:
  0.0 180.4 jit_solution(4787722068686721112)
XLA Ops:
  6.5 0.0 copy-start
  6.5 0.0 all-gather.2.cloned.1.call-start
  6.5 1.3 copy.10
  7.9 0.7 select_reduce_fusion
  8.6 0.8 broadcast_select_fusion
  9.5 0.0 all-gather.2.cloned.1.call-update
  9.5 1.3 dynamic_slice.3
  10.8 1.4 gather_fusion
  12.2 0.7 compare_and_fusion
  12.9 100.7 %all-gather.2.cloned.1.call-done = bf16[16384,512]{0,1:T(8,128)(2,1)} async-done(((bf16[512,512]{0,1:T(8,128)(2,1)}), bf16[16384,512]{0,1:T(8,128)(2,1)}) %all-gather.2.cloned.1.call-update) | async-done | bytes 16777232 | tf_op jit(solution)/shard_map/all_gather | solution.py:42
  113.6 14.0 %copy.14 = bf16[64,16,8,1024]{3,2,0,1:T(8,128)(2,1)} copy(bf16[64,16,8,1024]{3,2,1,0:T(8,128)(2,1)} %bitcast.24) | data formatting | bytes 33554432 | tf_op jit(solution)/shard_map/reshape | solution.py:43
  127.6 10.4 %gather_fusion.1 = bf16[8,1024,512]{1,2,0:T(8,128)(2,1)} fusion(bf16[16,1024,512]{1,2,0:T(8,128)(2,1)} %bitcast.23, s32[1024]{0:T(1024)S(1)} %pad_clamp_fusion), kind=kCustom, calls=%fused_computation.1 | custom fusion | bytes 16777248 | tf_op jit(solution)/shard_map/jit(_take)/gather | solution.py:44
  138.0 10.7 %convert_reduce_fusion = bf16[512,512]{1,0:T(8,128)(2,1)S(1)} fusion(pred[8]{0:T(512)(128)(4,1)S(1)} %get-tuple-element.6, bf16[1,8,512,1024]{3,2,1,0:T(8,128)(2,1)} %param.7, bf16[8,1024,512]{1,2,0:T(8,128)(2,1)} %gather_fusion.1, pred[8]{0:T(512)(128)(4,1)S(1)} %get-tuple-element.5), kind=kOutput, calls=%fused_computation.5 | convolution fusion | flops 4307288064 | bytes 17301520 | tf_op jit(solution)/shard_map/kri,kic->krc/dot_general | solution.py:46
  148.7 0.0 copy-done
  148.7 0.5 convolution_select_fusion
  149.2 23.6 %all_to_all.5 = f32[8,512,64]{1,2,0:T(8,128)S(1)} all-to-all(f32[8,512,64]{1,2,0:T(8,128)S(1)} %bitcast.25), channel_id=1, replica_groups=mesh['fam'=8,'owner'=32] {'fam'}, dimensions={0} | all-to-all | bytes 2097152 | tf_op jit(solution)/shard_map/all_to_all | solution.py:15
  172.8 0.7 reduce_sum.29
  (5 shorter events, 0.0 us)
Async XLA Ops:
  6.5 142.2 %copy-start = (bf16[1,512,512]{2,1,0:T(8,128)(2,1)S(1)}, bf16[1,512,512]{2,1,0:T(8,128)(2,1)}, u32[]{:S(2)}) copy-start(bf16[1,512,512]{2,1,0:T(8,128)(2,1)} %param.8) | copy-start | bytes 1572868
  6.5 107.1 %all-gather.2.cloned.1.call-start = ((), (), s32[]{:S(2)}) async-start(), calls=%async_computation.1 | async-start | bytes 17301504 | tf_op jit(solution)/shard_map/all_gather | solution.py:42
Sparse Core Ops, SparseCore 0:
  9.6 103.9 all-gather.1
where the time goes:
time: 181 us; the launch traced here: 180 us
  waiting for transfers between devices  101 us (56%)
  local copies, waits for them, and re-layouts  28.4 us (16%)
  blocking collectives  23.6 us (13%)
  between operations  13.5 us (7%)
  matrix products  11.2 us (6%)
  other arithmetic  2.99 us (2%)
    all_gather x1, waiting for transfers between devices, body(): whole = lax.all_gather(masked, 'owner', axis=0, tiled=True)  101 us
    all_to_all x1, blocking collectives, sent_and_summed(): parts = lax.all_to_all(in_blocks(value, dim, count), axis, 0, 0, tiled=True)  23.6 us
    reshape x1, local copies, waits for them, and re-layouts, body(): whole.reshape(whole.shape[0] // sector_len, sector_len, whole.shape[1])  14 us
    dot_general x1, matrix products, body(): jnp.einsum('kri,kic->krc', items, sources, preferred_element_type=jnp.flo...  10.7 us
    gather x1, local copies, waits for them, and re-layouts, body(): sources = jnp.take(stacked, source, axis=0)  10.4 us
  transfers between devices with their start and end apart: 1, of which 1 were waited for; matrix products, arithmetic and copies ran while one was open for 2% of the time, Pallas kernels for 0%

commit v1 on v0

v1 whole, which is shorter than its diff:
```python
import functools

import jax
import jax.numpy as jnp
from jax import lax
from jax.experimental import pallas as pl
from jax.experimental.pallas import tpu as pltpu
from jax.sharding import PartitionSpec as P

MESH = pl.DeviceIdType.MESH
S, SROW, COLS, KMAX, FAM = 16, 1024, 512, 8, 8
ROWS = 512
GROUPS = 2
CHUNK = ROWS // (4 * GROUPS)
LAG = 3
SPLIT_OWN, SPLIT_OPPOSITE = 8, 10
PARTS = 2
LINKS = ("z+", "z-", "y+", "y-", "x+", "x-")


def sender_label(link, label):
    dq, dz, h, j = label
    if link == "z+":
        return (0, dz - 1, h, j)
    if link == "z-":
        return (0, -3 if dz == 4 else dz + 1, h, j)
    if link[0] == "y":
        return (0, dz, h, j)
    if link == "x+":
        return (dq, dz, h, (j - 1) % 4)
    return (dq, dz, h, (j + 1) % 4)


def schedule():
    own = [(dz, h) for dz in (-1, 1, -2, 2, -3, 3, 4) for h in range(GROUPS)][:SPLIT_OWN]
    opposite = [(dz, h) for dz in (0, -1, 1, -2, 2, -3, 3, 4) for h in range(GROUPS)][:SPLIT_OPPOSITE]
    arrived = {(0, 0, h, j): -LAG for h in range(GROUPS) for j in range(4)}
    todo = {}
    for dq in (0, 1):
        for dz in range(-3, 5):
            if (dq, dz) == (0, 0):
                continue
            for h in range(GROUPS):
                split = (dz, h) in (opposite if dq else own)
                for j in range(4):
                    if split and j % 2:
                        links = ("x+",) if j == 1 else ("x-",)
                    elif dq:
                        links = ("y+", "y-")
                    elif dz == 4:
                        links = ("z+", "z-")
                    else:
                        links = ("z+",) if dz > 0 else ("z-",)
                    todo[(dq, dz, h, j)] = links

    def order(label):
        dq, dz, h, j = label
        ahead = 0
        if dq == 0:
            ahead += (4 - abs(dz)) * 10 + 3
        if j == 0 and (dz, h) in (opposite if dq else own):
            ahead += 2
        if dq == 0 and (dz, h) in opposite:
            ahead += 2
        return (-ahead, abs(dz), h, j)

    rounds = []
    while todo:
        now = {}
        for link in LINKS:
            ready = [
                label
                for label, links in todo.items()
                if link in links and arrived.get(sender_label(link, label), 1 << 20) <= len(rounds) - LAG
            ]
            if ready:
                now[link] = min(ready, key=order)
                del todo[now[link]]
        for label in now.values():
            arrived[label] = len(rounds)
        rounds.append(now)
    return rounds


ROUNDS = schedule()


def kernel(
    sources_ref,
    counts_ref,
    used_ref,
    wave_hbm,
    left_hbm,
    right_hbm,
    out_ref,
    gathered,
    wave,
    left,
    right,
    right_t,
    sums,
    outgoing,
    incoming,
    load_sem,
    send_sem,
    recv_sem,
    core_send_sem,
    core_recv_sem,
    fam_send_sem,
    fam_recv_sem,
):
    f = lax.axis_index("fam")
    o = lax.axis_index("owner")
    x, yh = lax.rem(f, 4), f // 4
    core, z, yl = lax.rem(o, 2), lax.rem(o // 2, 8), o // 16
    y = yh * 2 + yl
    sector = o // 2

    def device(dx, dy, dz, other=False):
        nx, ny, nz = lax.rem(x + dx + 4, 4), lax.rem(y + dy + 4, 4), lax.rem(z + dz + 8, 8)
        c = 1 - core if other else core
        return ((ny // 2) * 4 + nx, (lax.rem(ny, 2) * 8 + nz) * 2 + c)

    loads = [
        pltpu.make_async_copy(wave_hbm, wave, load_sem.at[0]),
        pltpu.make_async_copy(right_hbm, right, load_sem.at[1]),
        pltpu.make_async_copy(left_hbm, left, load_sem.at[2]),
    ]
    for load in loads:
        load.start()

    barrier = pltpu.get_barrier_semaphore()
    fam_steps = [(dx, dy) for dy in (0, 2) for dx in range(4) if (dx, dy) != (0, 0)]
    greeted = [(dx, dy, 0, False) for dx, dy in fam_steps]
    greeted += [(0, 1, 0, False), (0, -1, 0, False), (0, 0, 1, False), (0, 0, -1, False), (0, 0, 0, True)]
    for where in greeted:
        pl.semaphore_signal(barrier, inc=1, device_id=device(*where), device_id_type=MESH)

    def chunk_at(label):
        dq, dz, h, j = label
        q = 1 - yl if dq else yl
        a = q * 8 + lax.rem(z + dz + 8, 8)
        i = 4 * h + lax.rem(x + j, 4)
        return gathered.at[a, pl.ds(pl.multiple_of(core * ROWS + i * CHUNK, CHUNK), CHUNK)]

    own = pl.ds(pl.multiple_of(core * ROWS, ROWS), ROWS)
    used_here = used_ref[sector] - core * ROWS
    loads[0].wait()
    row = lax.broadcasted_iota(jnp.int32, (ROWS, COLS), 0)
    gathered[sector, own, :] = jnp.where(row < used_here, wave[...].astype(jnp.float32), 0.0).astype(jnp.bfloat16)

    pl.semaphore_wait(barrier, len(greeted))

    targets = {
        "z+": (0, 0, -1), "z-": (0, 0, 1), "y+": (0, -1, 0), "y-": (0, 1, 0), "x+": (-1, 0, 0), "x-": (1, 0, 0),
    }

    def to_other_core(part):
        pltpu.make_async_remote_copy(
            src_ref=part, dst_ref=part, send_sem=core_send_sem, recv_sem=core_recv_sem,
            device_id=device(0, 0, 0, True), device_id_type=MESH,
        ).start()

    for step in range(len(ROUNDS) + LAG):
        if step >= LAG:
            for link, label in ROUNDS[step - LAG].items():
                part = chunk_at(label)
                pltpu.make_async_remote_copy(
                    src_ref=part, dst_ref=part, send_sem=send_sem, recv_sem=recv_sem.at[step - LAG, LINKS.index(link)],
                    device_id=device(*targets[link]), device_id_type=MESH,
                ).wait_recv()
        if step < len(ROUNDS):
            for link, label in ROUNDS[step].items():
                part = chunk_at(sender_label(link, label))
                pltpu.make_async_remote_copy(
                    src_ref=part, dst_ref=part, send_sem=send_sem, recv_sem=recv_sem.at[step, LINKS.index(link)],
                    device_id=device(*targets[link]), device_id_type=MESH,
                ).start()
        if step == 0:
            to_other_core(gathered.at[sector, own])
            loads[1].wait()
            right_t[...] = right[0].astype(jnp.float32).T.astype(jnp.bfloat16)
        if step >= LAG:
            for label in ROUNDS[step - LAG].values():
                to_other_core(chunk_at(label))
    loads[2].wait()
    half = gathered.at[pl.ds(0, S // 2)]
    pltpu.make_async_copy(half, half, core_recv_sem).wait()

    live_slots = counts_ref[f, sector]
    depth = ROWS // PARTS
    for part in range(PARTS):

        def add_slot(k, carry, part=part):
            a = sources_ref[f, k, sector]
            product = jnp.dot(
                left[0, k, part * depth : (part + 1) * depth, :],
                gathered[a],
                preferred_element_type=jnp.float32,
            )
            slot = k + jnp.zeros((depth, COLS), jnp.int32)
            sums[...] += jnp.where(slot < live_slots, product, 0.0)
            return carry

        sums[...] = jnp.zeros_like(sums)
        lax.fori_loop(0, KMAX, add_slot, 0)
        turned = lax.dot_general(
            right_t[...], sums[...].astype(jnp.bfloat16), (((1,), (1,)), ((), ())), preferred_element_type=jnp.float32
        )
        outgoing[part] = turned.astype(jnp.bfloat16).reshape(FAM, COLS // FAM, depth)
        for dx, dy in fam_steps:
            there = device(dx, dy, 0)
            pltpu.make_async_remote_copy(
                src_ref=outgoing.at[part, there[0]], dst_ref=incoming.at[part, f], send_sem=fam_send_sem,
                recv_sem=fam_recv_sem.at[part], device_id=there, device_id_type=MESH,
            ).start()

    for part in range(PARTS):
        others = incoming.at[part, pl.ds(0, FAM - 1)]
        pltpu.make_async_copy(others, others, fam_recv_sem.at[part]).wait()
        incoming[part, f] = outgoing[part, f]
        total = jnp.sum(incoming[part].astype(jnp.float32), axis=0)
        column = part * depth + lax.broadcasted_iota(jnp.int32, total.shape, 1)
        out_ref[:, part * depth : (part + 1) * depth] = jnp.where(column < used_here, total, 0.0).astype(jnp.bfloat16)

    for part in range(PARTS):
        others = outgoing.at[part, pl.ds(0, FAM - 1)]
        pltpu.make_async_copy(others, others, fam_send_sem).wait()
    sent = gathered.at[pl.ds(0, S - 1), pl.ds(0, ROWS)]
    pltpu.make_async_copy(sent, sent, send_sem).wait()
    pltpu.make_async_copy(half, half, core_send_sem).wait()


def body(wavefunction, left_blocks, right_blocks, term_sources, term_counts, sector_rows):
    vmem = pl.BlockSpec(memory_space=pltpu.VMEM)
    smem = pl.BlockSpec(memory_space=pltpu.SMEM)
    anywhere = pl.BlockSpec(memory_space=pl.ANY)
    turned = pl.pallas_call(
        kernel,
        out_shape=jax.ShapeDtypeStruct((COLS // FAM, ROWS), jnp.bfloat16),
        in_specs=[smem, smem, smem, anywhere, anywhere, anywhere],
        out_specs=vmem,
        scratch_shapes=[
            pltpu.VMEM((S, SROW, COLS), jnp.bfloat16),
            pltpu.VMEM((ROWS, COLS), jnp.bfloat16),
            pltpu.VMEM((1, KMAX, ROWS, SROW), jnp.bfloat16),
            pltpu.VMEM((1, COLS, COLS), jnp.bfloat16),
            pltpu.VMEM((COLS, COLS), jnp.bfloat16),
            pltpu.VMEM((ROWS // PARTS, COLS), jnp.float32),
            pltpu.VMEM((PARTS, FAM, COLS // FAM, ROWS // PARTS), jnp.bfloat16),
            pltpu.VMEM((PARTS, FAM, COLS // FAM, ROWS // PARTS), jnp.bfloat16),
            pltpu.SemaphoreType.DMA((3,)),
            pltpu.SemaphoreType.DMA,
            pltpu.SemaphoreType.DMA((len(ROUNDS), len(LINKS))),
            pltpu.SemaphoreType.DMA,
            pltpu.SemaphoreType.DMA,
            pltpu.SemaphoreType.DMA,
            pltpu.SemaphoreType.DMA((PARTS,)),
        ],
        compiler_params=pltpu.CompilerParams(
            collective_id=0, has_side_effects=True, vmem_limit_bytes=56 * 2**20
        ),
        cost_estimate=pl.CostEstimate(flops=2 * KMAX * ROWS * SROW * COLS, bytes_accessed=9 * 2**20, transcendentals=0),
        name="gather_multiply_scatter",
    )(jnp.swapaxes(term_sources, 1, 2), term_counts, sector_rows, wavefunction, left_blocks, right_blocks)
    return turned.T


def solution(mesh):
    return jax.shard_map(
        body,
        mesh=mesh,
        in_specs=(
            P("owner", None),
            P("fam", None, "owner", None),
            P("fam", None, None),
            P(),
            P(),
            P(),
        ),
        out_specs=P("owner", "fam"),
        check_vma=False,
    )
```

time: 181 us -> 66.7 us (0.37)
  waiting for transfers between devices: 101 us -> 0 us
  Pallas kernels: 0 us -> 65 us
  local copies, waits for them, and re-layouts: 28.4 us -> 1.47 us
  blocking collectives: 23.6 us -> 0 us
  between operations: 13.5 us -> 0.01 us
  matrix products: 11.2 us -> 0 us
  other arithmetic: 2.99 us -> 0 us
    all_gather x1 -> x0, waiting for transfers between devices: 101 us -> none  [body(): whole = lax.all_gather(masked, 'owner', axis=0, tiled=True)]
    pallas_call x0 -> x1, Pallas kernels: none -> 65 us  [body(): pl.pallas_call(kernel, out_shape=jax.ShapeDtypeStruct((COLS // FAM, ROWS)...]
    all_to_all x1 -> x0, blocking collectives: 23.6 us -> none  [sent_and_summed(): parts = lax.all_to_all(in_blocks(value, dim, count), axis, 0, 0, tiled=True)]
    reshape x1 -> x0, local copies, waits for them, and re-layouts: 14 us -> none  [body(): whole.reshape(whole.shape[0] // sector_len, sector_len, whole.shape[1])]
    gather x2 -> x0, local copies, waits for them, and re-layouts: 11.8 us -> none  [the longest x1 10.4 us: body(): sources = jnp.take(stacked, source, axis=0)]
    dot_general x2 -> x0, matrix products: 11.2 us -> none  [the longest x1 10.7 us: body(): jnp.einsum('kri,kic->krc', items, sources, preferred_element_type=jnp.flo...]
  transfers between devices with their start and end apart: 1 -> 0, of which waited for: 1 -> 0; matrix products, arithmetic and copies ran while one was open for 2% -> 0% of each run, Pallas kernels for 0% -> 0%
where the time goes in v1:
time: 66.7 us; the launch traced here: 66.4 us
  Pallas kernels  65 us (97%)
  local copies, waits for them, and re-layouts  1.47 us (2%)
    pallas_call x1, Pallas kernels, body(): pl.pallas_call(kernel, out_shape=jax.ShapeDtypeStruct((COLS // FAM, ROWS)...  65 us
    unnamed x1, local copies, waits for them, and re-layouts  1.47 us

profile of v1, /device:TPU:1, one launch (start us, length us, event | category | flops | bytes accessed | tf_op | source)
XLA Modules:
  0.0 66.4 jit_solution(9988207374206217778)
XLA Ops:
  0.0 65.0 %gather_multiply_scatter.1 = bf16[64,512]{1,0:T(8,128)(2,1)} custom-call(s32[8,8,16]{2,1,0:T(8,128)} %bitcast.3, s32[8,16]{1,0:T(8,128)} %counts_ref.1, s32[16]{0:T(128)} %used_ref.1, bf16[512,512]{1,0:T(8,128)(2,1)} %wave_hbm.1, bf16[1,8,512,1024]{3,2,1,0:T(8,128)(2,1)} %left_hbm.1, bf16[1,512,512]{2,1,0:T(8,128)(2,1)} %right_hbm.1), custom_call_target="tpu_custom_call" | custom-call | flops 4294967296 | bytes 9437184 | tf_op jit(solution)/shard_map/gather_multiply_scatter/pallas_call | solution.py:238
  65.0 1.5 %copy.8 = bf16[512,64]{0,1:T(8,128)(2,1)} copy(bf16[512,64]{0,1:T(8,128)(2,1)} %bitcast.2) | data formatting | bytes 131072

commit v2 on v1

--- a/solution.py
+++ b/solution.py
@@ -12,7 +12,7 @@
 ROWS = 512
 GROUPS = 2
 CHUNK = ROWS // (4 * GROUPS)
-LAG = 3
+LAG = 4
 SPLIT_OWN, SPLIT_OPPOSITE = 8, 10
 PARTS = 2
 LINKS = ("z+", "z-", "y+", "y-", "x+", "x-")
@@ -203,7 +203,7 @@
             return carry
 
         sums[...] = jnp.zeros_like(sums)
-        lax.fori_loop(0, KMAX, add_slot, 0)
+        lax.fori_loop(0, KMAX, add_slot, 0, unroll=True)
         turned = lax.dot_general(
             right_t[...], sums[...].astype(jnp.bfloat16), (((1,), (1,)), ((), ())), preferred_element_type=jnp.float32
         )

time: 66.7 us -> 62.2 us (0.933)
  Pallas kernels: 65 us -> 60.5 us
    pallas_call x1, Pallas kernels: 65 us -> 60.5 us  [body(): pl.pallas_call(kernel, out_shape=jax.ShapeDtypeStruct((COLS // FAM, ROWS)...]
where the time goes in v2:
time: 62.2 us; the launch traced here: 62 us
  Pallas kernels  60.5 us (97%)
  local copies, waits for them, and re-layouts  1.47 us (2%)
    pallas_call x1, Pallas kernels, body(): pl.pallas_call(kernel, out_shape=jax.ShapeDtypeStruct((COLS // FAM, ROWS)...  60.5 us
    unnamed x1, local copies, waits for them, and re-layouts  1.47 us

profile of v2, /device:TPU:1, one launch (start us, length us, event | category | flops | bytes accessed | tf_op | source)
XLA Modules:
  0.0 62.0 jit_solution(17666076448980823321)
XLA Ops:
  0.0 60.5 %gather_multiply_scatter.1 = bf16[64,512]{1,0:T(8,128)(2,1)} custom-call(s32[8,8,16]{2,1,0:T(8,128)} %bitcast.3, s32[8,16]{1,0:T(8,128)} %counts_ref.1, s32[16]{0:T(128)} %used_ref.1, bf16[512,512]{1,0:T(8,128)(2,1)} %wave_hbm.1, bf16[1,8,512,1024]{3,2,1,0:T(8,128)(2,1)} %left_hbm.1, bf16[1,512,512]{2,1,0:T(8,128)(2,1)} %right_hbm.1), custom_call_target="tpu_custom_call" | custom-call | flops 4294967296 | bytes 9437184 | tf_op jit(solution)/shard_map/gather_multiply_scatter/pallas_call | solution.py:238
  60.5 1.5 %copy.8 = bf16[512,64]{0,1:T(8,128)(2,1)} copy(bf16[512,64]{0,1:T(8,128)(2,1)} %bitcast.2) | data formatting | bytes 131072

commit v3 on v2

v3 whole, which is shorter than its diff:
```python
import functools

import jax
import jax.numpy as jnp
from jax import lax
from jax.experimental import pallas as pl
from jax.experimental.pallas import tpu as pltpu
from jax.sharding import PartitionSpec as P

MESH = pl.DeviceIdType.MESH
S, SROW, COLS, KMAX, FAM = 16, 1024, 512, 8, 8
ROWS = 512
GROUPS = 2
CHUNK = ROWS // (4 * GROUPS)
LAG = 3
PARTS = 2
DEPTH = ROWS // PARTS
LINKS = ((0, 0, 1), (0, 0, -1), (0, 1, 0), (0, -1, 0), (1, 0, 0), (-1, 0, 0))

ROUNDS = (
    (36, 20, 95, 92, -1, -1),
    (33, 18, 88, 89, -1, -1),
    (32, 16, 90, 94, -1, -1),
    (38, 84, 100, 91, 93, 39),
    (34, 10, 82, 97, 19, 17),
    (44, 21, 80, 96, 37, 35),
    (41, 23, 103, 102, 101, 87),
    (40, 12, 98, 74, 85, 81),
    (43, 2, 83, 99, 11, 47),
    (45, 8, 105, 108, 22, 9),
    (49, 4, 104, 76, 13, 86),
    (109, 15, 107, 66, 75, 46),
    (48, 14, 73, 72, 42, 111),
    (110, 60, 113, 77, 5, 7),
    (54, 0, 68, 79, 50, 106),
    (56, 64, 78, 112, 67, 51),
    (116, 3, 69, 124, 6, 1),
    (62, 58, 114, 71, 55, 63),
    (53, 70, 120, 115, 65, 59),
    (57, 122, 52, 118, 117, 119),
    (121, 123, 126, 127, 125, 61),
)


def parts_of(label):
    return label // 64, label // 8 % 8 - 3, label // 4 % 2, label % 4


def sender_parts(link, label):
    dq, dz, h, j = parts_of(label)
    dx, dy, step = LINKS[link]
    return (dq + dy) % 2, (dz - step + 3) % 8 - 3, h, (j - dx) % 4


def kernel(
    sources_ref,
    counts_ref,
    used_ref,
    wave_hbm,
    left_hbm,
    right_hbm,
    out_ref,
    gathered,
    left,
    right,
    right_t,
    sums,
    half_out,
    half_in,
    outgoing,
    incoming,
    load_sem,
    send_sem,
    recv_sem,
    left_send_sem,
    left_recv_sem,
    half_send_sem,
    half_recv_sem,
    fam_send_sem,
    fam_recv_sem,
):
    f = lax.axis_index("fam")
    o = lax.axis_index("owner")
    x, yh = lax.rem(f, 4), f // 4
    core, z, yl = lax.rem(o, 2), lax.rem(o // 2, 8), o // 16
    y = yh * 2 + yl
    sector = o // 2

    def device(dx, dy, dz, other=False):
        nx, ny, nz = lax.rem(x + dx + 4, 4), lax.rem(y + dy + 4, 4), lax.rem(z + dz + 8, 8)
        c = 1 - core if other else core
        return ((ny // 2) * 4 + nx, (lax.rem(ny, 2) * 8 + nz) * 2 + c)

    mine = pl.ds(pl.multiple_of(core * ROWS, ROWS), ROWS)
    others = pl.ds(pl.multiple_of((1 - core) * ROWS, ROWS), ROWS)
    loads = [
        pltpu.make_async_copy(wave_hbm, gathered.at[sector], load_sem.at[0]),
        pltpu.make_async_copy(right_hbm, right, load_sem.at[1]),
        pltpu.make_async_copy(left_hbm.at[0, :, :, mine], left.at[0], load_sem.at[2]),
    ]
    for load in loads:
        load.start()

    barrier = pltpu.get_barrier_semaphore()
    fam_steps = [(dx, dy) for dy in (0, 2) for dx in range(4) if (dx, dy) != (0, 0)]
    greeted = [(dx, dy, 0, False) for dx, dy in fam_steps]
    greeted += [(0, 1, 0, False), (0, -1, 0, False), (0, 0, 1, False), (0, 0, -1, False), (0, 0, 0, True)]
    for where in greeted:
        pl.semaphore_signal(barrier, inc=1, device_id=device(*where), device_id_type=MESH)

    def chunk_rows(h, j):
        return pl.ds(pl.multiple_of((4 * h + lax.rem(x + j, 4)) * CHUNK, CHUNK), CHUNK)

    def chunk_at(dq, dz, h, j):
        q = 1 - yl if dq else yl
        return gathered.at[q * 8 + lax.rem(z + dz + 8, 8), chunk_rows(h, j)]

    pl.semaphore_wait(barrier, len(greeted))

    def arrival(step, link, source, part):
        dx, dy, dz = LINKS[link]
        return pltpu.make_async_remote_copy(
            src_ref=source, dst_ref=part, send_sem=send_sem, recv_sem=recv_sem.at[step, link],
            device_id=device(-dx, -dy, -dz), device_id_type=MESH,
        )

    to_core = pltpu.make_async_remote_copy(
        src_ref=left_hbm.at[0, :, :, others], dst_ref=left.at[1], send_sem=left_send_sem, recv_sem=left_recv_sem,
        device_id=device(0, 0, 0, True), device_id_type=MESH,
    )
    live_slots = counts_ref[f, sector]
    arrives = {parts_of(label): (step, link) for step, row in enumerate(ROUNDS) for link, label in enumerate(row) if label >= 0}

    def wait_for(chunk):
        if chunk in arrives:
            part = chunk_at(*chunk)
            arrival(*arrives.pop(chunk), part, part).wait_recv()

    for step in range(len(ROUNDS)):
        if step == LAG:
            loads[0].wait()
        sends = [(link, sender_parts(link, label)) for link, label in enumerate(ROUNDS[step]) if label >= 0]
        for link, chunk in sorted(sends, key=lambda send: send[1] in arrives):
            wait_for(chunk)
            part = chunk_at(*chunk)
            source = wave_hbm.at[chunk_rows(*chunk[2:])] if chunk[:2] == (0, 0) and step < LAG else part
            arrival(step, link, source, part).start()
        if step == 0:
            to_core.start()
            loads[1].wait()
            right_t[...] = right[0].astype(jnp.float32).T.astype(jnp.bfloat16)
        if step == len(ROUNDS) - 8:
            loads[2].wait()
            to_core.wait_recv()
        k = step - (len(ROUNDS) - 8)
        if 0 <= k < KMAX:
            column = lax.broadcasted_iota(jnp.int32, (1, ROWS), 1)
            used = jnp.where(column + core * ROWS < used_ref[sources_ref[f, k, sector]], 1.0, 0.0)
            used = jnp.where(k + jnp.zeros_like(column) < live_slots, used, 0.0).astype(jnp.bfloat16)
            for side in range(2):
                left[side, k] = left[side, k] * used

    for chunk in sorted(arrives, key=arrives.get):
        wait_for(chunk)

    def product(side, part):
        def add_slot(k, carry):
            a = sources_ref[f, k, sector]
            slot = k + jnp.zeros((DEPTH, COLS), jnp.int32)
            term = jnp.dot(
                left[side, k, part * DEPTH : (part + 1) * DEPTH, :], gathered[a], preferred_element_type=jnp.float32
            )
            sums[...] += jnp.where(slot < live_slots, term, 0.0)
            return carry

        sums[...] = jnp.zeros_like(sums)
        lax.fori_loop(0, KMAX, add_slot, 0, unroll=True)
        return sums[...]

    halves = [
        pltpu.make_async_remote_copy(
            src_ref=half_out.at[part], dst_ref=half_in.at[part], send_sem=half_send_sem.at[part],
            recv_sem=half_recv_sem.at[part], device_id=device(0, 0, 0, True), device_id_type=MESH,
        )
        for part in range(PARTS)
    ]
    def for_other_core(part):
        half_out[part] = product(1, part).astype(jnp.bfloat16)
        halves[part].start()

    def for_families(part):
        own_half = product(0, part)
        halves[part].wait_recv()
        partial_sum = (own_half + half_in[part].astype(jnp.float32)).astype(jnp.bfloat16)
        turned = lax.dot_general(
            right_t[...], partial_sum, (((1,), (1,)), ((), ())), preferred_element_type=jnp.float32
        )
        outgoing[part] = turned.astype(jnp.bfloat16).reshape(FAM, COLS // FAM, DEPTH)
        for dx, dy in fam_steps:
            there = device(dx, dy, 0)
            pltpu.make_async_remote_copy(
                src_ref=outgoing.at[part, there[0]], dst_ref=incoming.at[part, f], send_sem=fam_send_sem,
                recv_sem=fam_recv_sem.at[part], device_id=there, device_id_type=MESH,
            ).start()

    for_other_core(0)
    for part in range(PARTS):
        if part + 1 < PARTS:
            for_other_core(part + 1)
        for_families(part)

    for part in range(PARTS):
        rest = incoming.at[part, pl.ds(0, FAM - 1)]
        pltpu.make_async_copy(rest, rest, fam_recv_sem.at[part]).wait()
        incoming[part, f] = outgoing[part, f]
        total = jnp.sum(incoming[part].astype(jnp.float32), axis=0)
        row = core * ROWS + part * DEPTH + lax.broadcasted_iota(jnp.int32, total.shape, 1)
        out_ref[:, part * DEPTH : (part + 1) * DEPTH] = jnp.where(row < used_ref[sector], total, 0.0).astype(jnp.bfloat16)

    for part in range(PARTS):
        rest = outgoing.at[part, pl.ds(0, FAM - 1)]
        pltpu.make_async_copy(rest, rest, fam_send_sem).wait()
        halves[part].wait_send()
    to_core.wait_send()
    sent = gathered.at[pl.ds(0, S - 1)]
    pltpu.make_async_copy(sent, sent, send_sem).wait()


def body(wavefunction, left_blocks, right_blocks, term_sources, term_counts, sector_rows):
    vmem = pl.BlockSpec(memory_space=pltpu.VMEM)
    smem = pl.BlockSpec(memory_space=pltpu.SMEM)
    anywhere = pl.BlockSpec(memory_space=pl.ANY)
    turned = pl.pallas_call(
        kernel,
        out_shape=jax.ShapeDtypeStruct((COLS // FAM, ROWS), jnp.bfloat16),
        in_specs=[smem, smem, smem, anywhere, anywhere, anywhere],
        out_specs=vmem,
        scratch_shapes=[
            pltpu.VMEM((S, ROWS, COLS), jnp.bfloat16),
            pltpu.VMEM((2, KMAX, ROWS, ROWS), jnp.bfloat16),
            pltpu.VMEM((1, COLS, COLS), jnp.bfloat16),
            pltpu.VMEM((COLS, COLS), jnp.bfloat16),
            pltpu.VMEM((DEPTH, COLS), jnp.float32),
            pltpu.VMEM((PARTS, DEPTH, COLS), jnp.bfloat16),
            pltpu.VMEM((PARTS, DEPTH, COLS), jnp.bfloat16),
            pltpu.VMEM((PARTS, FAM, COLS // FAM, DEPTH), jnp.bfloat16),
            pltpu.VMEM((PARTS, FAM, COLS // FAM, DEPTH), jnp.bfloat16),
            pltpu.SemaphoreType.DMA((3,)),
            pltpu.SemaphoreType.DMA,
            pltpu.SemaphoreType.DMA((len(ROUNDS), len(LINKS))),
            pltpu.SemaphoreType.DMA,
            pltpu.SemaphoreType.DMA,
            pltpu.SemaphoreType.DMA((PARTS,)),
            pltpu.SemaphoreType.DMA((PARTS,)),
            pltpu.SemaphoreType.DMA,
            pltpu.SemaphoreType.DMA((PARTS,)),
        ],
        compiler_params=pltpu.CompilerParams(
            collective_id=0, has_side_effects=True, vmem_limit_bytes=56 * 2**20
        ),
        cost_estimate=pl.CostEstimate(flops=2 * KMAX * ROWS * SROW * COLS, bytes_accessed=9 * 2**20, transcendentals=0),
        name="gather_multiply_scatter",
    )(jnp.swapaxes(term_sources, 1, 2), term_counts, sector_rows, wavefunction, left_blocks, right_blocks)
    return turned.T


def solution(mesh):
    return jax.shard_map(
        body,
        mesh=mesh,
        in_specs=(
            P("owner", None),
            P("fam", None, "owner", None),
            P("fam", None, None),
            P(),
            P(),
            P(),
        ),
        out_specs=P("owner", "fam"),
        check_vma=False,
    )
```

time: 62.2 us -> 59.3 us (0.953)
  Pallas kernels: 60.5 us -> 57.6 us
    pallas_call x1, Pallas kernels: 60.5 us -> 57.6 us  [body(): pl.pallas_call(kernel, out_shape=jax.ShapeDtypeStruct((COLS // FAM, ROWS)...]
where the time goes in v3:
time: 59.3 us; the launch traced here: 59 us
  Pallas kernels  57.6 us (97%)
  local copies, waits for them, and re-layouts  1.47 us (2%)
    pallas_call x1, Pallas kernels, body(): pl.pallas_call(kernel, out_shape=jax.ShapeDtypeStruct((COLS // FAM, ROWS)...  57.6 us
    unnamed x1, local copies, waits for them, and re-layouts  1.47 us

profile of v3, /device:TPU:1, one launch (start us, length us, event | category | flops | bytes accessed | tf_op | source)
XLA Modules:
  0.0 59.0 jit_solution(4523547616433935263)
XLA Ops:
  0.0 57.6 %gather_multiply_scatter.1 = bf16[64,512]{1,0:T(8,128)(2,1)} custom-call(s32[8,8,16]{2,1,0:T(8,128)} %bitcast.3, s32[8,16]{1,0:T(8,128)} %counts_ref.1, s32[16]{0:T(128)} %used_ref.1, bf16[512,512]{1,0:T(8,128)(2,1)} %wave_hbm.1, bf16[1,8,512,1024]{3,2,1,0:T(8,128)(2,1)} %left_hbm.1, bf16[1,512,512]{2,1,0:T(8,128)(2,1)} %right_hbm.1), custom_call_target="tpu_custom_call" | custom-call | flops 4294967296 | bytes 9437184 | tf_op jit(solution)/shard_map/gather_multiply_scatter/pallas_call | solution.py:233
  57.6 1.5 %copy.8 = bf16[512,64]{0,1:T(8,128)(2,1)} copy(bf16[512,64]{0,1:T(8,128)(2,1)} %bitcast.2) | data formatting | bytes 131072

commit v4 on v3

v4 whole, which is shorter than its diff:
```python
import functools

import jax
import jax.numpy as jnp
from jax import lax
from jax.experimental import pallas as pl
from jax.experimental.pallas import tpu as pltpu
from jax.sharding import PartitionSpec as P

MESH = pl.DeviceIdType.MESH
S, SROW, COLS, KMAX, FAM = 16, 1024, 512, 8, 8
ROWS = 512
CHUNK = ROWS // 4
WIDTH = COLS // 2
LAG = 3
PARTS = 4
MASK_AT, FIRST_AT = 9, 18
DEPTH = ROWS // PARTS
LINKS = ((0, 0, 1), (0, 0, -1), (0, 1, 0), (0, -1, 0), (1, 0, 0), (-1, 0, 0))

ROUNDS = (
    (36, 18, 88, 89, -1, -1),
    (35, 22, 95, 92, -1, -1),
    (32, 19, 90, 93, -1, -1),
    (97, 10, 82, 100, 37, 39),
    (43, 80, 99, 91, 23, 34),
    (98, 81, 96, 83, 16, 17),
    (105, 20, 33, 74, 11, 9),
    (51, 15, 101, 103, 40, 42),
    (104, 8, 87, 107, 94, 38),
    (113, 3, 73, 41, 106, 21),
    (109, 66, 115, 75, 48, 50),
    (59, 0, 79, 72, 102, 86),
    (121, 13, 49, 67, 114, 2),
    (56, 7, 85, 112, 110, 65),
    (117, 122, 64, 123, 76, 58),
    (44, 5, 77, 57, 1, 120),
    (118, 63, 71, 45, 111, 78),
    (47, 68, 53, 46, 84, 116),
    (108, 61, 69, 12, 6, 4),
    (126, 55, 54, 14, 119, 62),
    (125, 124, 52, 127, 60, 70),
)


def parts_of(label):
    return label // 64, label // 8 % 8 - 3, label // 4 % 2, label % 4


def sender_parts(link, label):
    dq, dz, h, j = parts_of(label)
    dx, dy, step = LINKS[link]
    return (dq + dy) % 2, (dz - step + 3) % 8 - 3, h, (j - dx) % 4


def kernel(
    sources_ref,
    counts_ref,
    used_ref,
    wave_hbm,
    left_hbm,
    right_hbm,
    out_ref,
    gathered_first,
    gathered_second,
    left,
    right,
    right_t,
    sums,
    first,
    half_out,
    half_in,
    outgoing,
    incoming,
    load_sem,
    send_sem,
    recv_sem,
    left_send_sem,
    left_recv_sem,
    half_send_sem,
    half_recv_sem,
    fam_send_sem,
    fam_recv_sem,
):
    gathered = (gathered_first, gathered_second)
    f = lax.axis_index("fam")
    o = lax.axis_index("owner")
    x, yh = lax.rem(f, 4), f // 4
    core, z, yl = lax.rem(o, 2), lax.rem(o // 2, 8), o // 16
    y = yh * 2 + yl
    sector = o // 2

    def device(dx, dy, dz, other=False):
        nx, ny, nz = lax.rem(x + dx + 4, 4), lax.rem(y + dy + 4, 4), lax.rem(z + dz + 8, 8)
        c = 1 - core if other else core
        return ((ny // 2) * 4 + nx, (lax.rem(ny, 2) * 8 + nz) * 2 + c)

    mine = pl.ds(pl.multiple_of(core * ROWS, ROWS), ROWS)
    others = pl.ds(pl.multiple_of((1 - core) * ROWS, ROWS), ROWS)
    loads = [
        pltpu.make_async_copy(wave_hbm.at[:, pl.ds(h * WIDTH, WIDTH)], gathered[h].at[sector], load_sem.at[h])
        for h in range(2)
    ] + [
        pltpu.make_async_copy(right_hbm, right, load_sem.at[3]),
        pltpu.make_async_copy(left_hbm.at[0, :, :, mine], left.at[0], load_sem.at[2]),
    ]
    for load in loads:
        load.start()

    barrier = pltpu.get_barrier_semaphore()
    fam_steps = [(dx, dy) for dy in (0, 2) for dx in range(4) if (dx, dy) != (0, 0)]
    greeted = [(1, 0, 0, False), (-1, 0, 0, False)]
    greeted += [(0, 1, 0, False), (0, -1, 0, False), (0, 0, 1, False), (0, 0, -1, False), (0, 0, 0, True)]
    for where in greeted:
        pl.semaphore_signal(barrier, inc=1, device_id=device(*where), device_id_type=MESH)

    def chunk_rows(j):
        return pl.ds(pl.multiple_of(lax.rem(x + j, 4) * CHUNK, CHUNK), CHUNK)

    def chunk_at(dq, dz, h, j):
        q = 1 - yl if dq else yl
        return gathered[h].at[q * 8 + lax.rem(z + dz + 8, 8), chunk_rows(j)]

    pl.semaphore_wait(barrier, len(greeted))

    def arrival(step, link, source, part):
        dx, dy, dz = LINKS[link]
        return pltpu.make_async_remote_copy(
            src_ref=source, dst_ref=part, send_sem=send_sem, recv_sem=recv_sem.at[step, link],
            device_id=device(-dx, -dy, -dz), device_id_type=MESH,
        )

    to_core = pltpu.make_async_remote_copy(
        src_ref=left_hbm.at[0, :, :, others], dst_ref=left.at[1], send_sem=left_send_sem, recv_sem=left_recv_sem,
        device_id=device(0, 0, 0, True), device_id_type=MESH,
    )
    live_slots = counts_ref[f, sector]

    def product(side, h, start, count):
        def add_slot(k, carry):
            a = sources_ref[f, k, sector]
            slot = k + jnp.zeros((count, WIDTH), jnp.int32)
            term = jnp.dot(left[side, k, start : start + count, :], gathered[h][a], preferred_element_type=jnp.float32)
            sums[:count] += jnp.where(slot < live_slots, term, 0.0)
            return carry

        sums[:count] = jnp.zeros((count, WIDTH), jnp.float32)
        lax.fori_loop(0, KMAX, add_slot, 0, unroll=True)
        return sums[:count]

    def times_right(h, partial_sum):
        return lax.dot_general(
            right_t[:, h * WIDTH : (h + 1) * WIDTH], partial_sum.astype(jnp.bfloat16), (((1,), (1,)), ((), ())),
            preferred_element_type=jnp.float32,
        )

    def half_copy(i, h, rows):
        return pltpu.make_async_remote_copy(
            src_ref=half_out.at[h, rows], dst_ref=half_in.at[h, rows], send_sem=half_send_sem.at[i],
            recv_sem=half_recv_sem.at[i], device_id=device(0, 0, 0, True), device_id_type=MESH,
        )

    halves = [half_copy(0, 0, pl.ds(0, ROWS))]
    halves += [half_copy(1 + part, 1, pl.ds(part * DEPTH, DEPTH)) for part in range(PARTS)]

    arrives = {parts_of(label): (step, link) for step, row in enumerate(ROUNDS) for link, label in enumerate(row) if label >= 0}

    def wait_for(chunk):
        if chunk in arrives:
            part = chunk_at(*chunk)
            arrival(*arrives.pop(chunk), part, part).wait_recv()

    for step in range(len(ROUNDS)):
        if step == LAG:
            loads[0].wait()
            loads[1].wait()
        sends = [(link, sender_parts(link, label)) for link, label in enumerate(ROUNDS[step]) if label >= 0]
        for link, chunk in sorted(sends, key=lambda send: send[1] in arrives):
            wait_for(chunk)
            part = chunk_at(*chunk)
            source = part
            if chunk[:2] == (0, 0) and step < LAG:
                source = wave_hbm.at[chunk_rows(chunk[3]), pl.ds(chunk[2] * WIDTH, WIDTH)]
            arrival(step, link, source, part).start()
        if step == 0:
            to_core.start()
            loads[2].wait()
            right_t[...] = right[0].astype(jnp.float32).T.astype(jnp.bfloat16)
        if step == MASK_AT:
            loads[3].wait()
            to_core.wait_recv()
        k = step - MASK_AT
        if 0 <= k < KMAX:
            column = core * ROWS + lax.broadcasted_iota(jnp.int32, (1, ROWS), 1)
            used = jnp.where(column < used_ref[sources_ref[f, k, sector]], 1.0, 0.0).astype(jnp.bfloat16)
            for side in range(2):
                left[side, k] = left[side, k] * used
        if step == FIRST_AT:
            for chunk in sorted(arrives, key=arrives.get):
                if chunk[2] == 0:
                    wait_for(chunk)
            half_out[0] = product(1, 0, 0, ROWS).astype(jnp.bfloat16)
            halves[0].start()
        if step == FIRST_AT + 1:
            product(0, 0, 0, ROWS)
        if step == FIRST_AT + 2:
            halves[0].wait_recv()
            first[...] = times_right(0, sums[...] + half_in[0].astype(jnp.float32))
    for chunk in sorted(arrives, key=arrives.get):
        wait_for(chunk)

    for part in range(PARTS):
        half_out[1, part * DEPTH : (part + 1) * DEPTH] = product(1, 1, part * DEPTH, DEPTH).astype(jnp.bfloat16)
        halves[1 + part].start()
    for part in range(PARTS):
        rows = slice(part * DEPTH, (part + 1) * DEPTH)
        own_half = product(0, 1, part * DEPTH, DEPTH)
        halves[1 + part].wait_recv()
        turned = first[:, rows] + times_right(1, own_half + half_in[1, rows].astype(jnp.float32))
        outgoing[part] = turned.astype(jnp.bfloat16).reshape(FAM, COLS // FAM, DEPTH)
        for dx, dy in fam_steps:
            there = device(dx, dy, 0)
            pltpu.make_async_remote_copy(
                src_ref=outgoing.at[part, there[0]], dst_ref=incoming.at[part, f], send_sem=fam_send_sem,
                recv_sem=fam_recv_sem.at[part], device_id=there, device_id_type=MESH,
            ).start()

    for part in range(PARTS):
        rest = incoming.at[part, pl.ds(0, FAM - 1)]
        pltpu.make_async_copy(rest, rest, fam_recv_sem.at[part]).wait()
        incoming[part, f] = outgoing[part, f]
        total = jnp.sum(incoming[part].astype(jnp.float32), axis=0)
        row = core * ROWS + part * DEPTH + lax.broadcasted_iota(jnp.int32, total.shape, 1)
        out_ref[:, part * DEPTH : (part + 1) * DEPTH] = jnp.where(row < used_ref[sector], total, 0.0).astype(jnp.bfloat16)

    for part in range(PARTS):
        rest = outgoing.at[part, pl.ds(0, FAM - 1)]
        pltpu.make_async_copy(rest, rest, fam_send_sem).wait()
    for half in halves:
        half.wait_send()
    to_core.wait_send()
    for half in gathered:
        sent = half.at[pl.ds(0, S - 1)]
        pltpu.make_async_copy(sent, sent, send_sem).wait()


def body(wavefunction, left_blocks, right_blocks, term_sources, term_counts, sector_rows):
    vmem = pl.BlockSpec(memory_space=pltpu.VMEM)
    smem = pl.BlockSpec(memory_space=pltpu.SMEM)
    anywhere = pl.BlockSpec(memory_space=pl.ANY)
    turned = pl.pallas_call(
        kernel,
        out_shape=jax.ShapeDtypeStruct((COLS // FAM, ROWS), jnp.bfloat16),
        in_specs=[smem, smem, smem, anywhere, anywhere, anywhere],
        out_specs=vmem,
        scratch_shapes=[
            pltpu.VMEM((S, ROWS, WIDTH), jnp.bfloat16),
            pltpu.VMEM((S, ROWS, WIDTH), jnp.bfloat16),
            pltpu.VMEM((2, KMAX, ROWS, ROWS), jnp.bfloat16),
            pltpu.VMEM((1, COLS, COLS), jnp.bfloat16),
            pltpu.VMEM((COLS, COLS), jnp.bfloat16),
            pltpu.VMEM((ROWS, WIDTH), jnp.float32),
            pltpu.VMEM((COLS, ROWS), jnp.float32),
            pltpu.VMEM((2, ROWS, WIDTH), jnp.bfloat16),
            pltpu.VMEM((2, ROWS, WIDTH), jnp.bfloat16),
            pltpu.VMEM((PARTS, FAM, COLS // FAM, DEPTH), jnp.bfloat16),
            pltpu.VMEM((PARTS, FAM, COLS // FAM, DEPTH), jnp.bfloat16),
            pltpu.SemaphoreType.DMA((4,)),
            pltpu.SemaphoreType.DMA,
            pltpu.SemaphoreType.DMA((len(ROUNDS), len(LINKS))),
            pltpu.SemaphoreType.DMA,
            pltpu.SemaphoreType.DMA,
            pltpu.SemaphoreType.DMA((1 + PARTS,)),
            pltpu.SemaphoreType.DMA((1 + PARTS,)),
            pltpu.SemaphoreType.DMA,
            pltpu.SemaphoreType.DMA((PARTS,)),
        ],
        compiler_params=pltpu.CompilerParams(
            collective_id=0, has_side_effects=True, vmem_limit_bytes=56 * 2**20
        ),
        cost_estimate=pl.CostEstimate(flops=2 * KMAX * ROWS * SROW * COLS, bytes_accessed=9 * 2**20, transcendentals=0),
        name="gather_multiply_scatter",
    )(jnp.swapaxes(term_sources, 1, 2), term_counts, sector_rows, wavefunction, left_blocks, right_blocks)
    return turned.T


def solution(mesh):
    return jax.shard_map(
        body,
        mesh=mesh,
        in_specs=(
            P("owner", None),
            P("fam", None, "owner", None),
            P("fam", None, None),
            P(),
            P(),
            P(),
        ),
        out_specs=P("owner", "fam"),
        check_vma=False,
    )
```

time: 59.3 us -> 58.1 us (0.980)
  Pallas kernels: 57.6 us -> 56.4 us
    pallas_call x1, Pallas kernels: 57.6 us -> 56.4 us  [body(): pl.pallas_call(kernel, out_shape=jax.ShapeDtypeStruct((COLS // FAM, ROWS)...]
where the time goes in v4:
time: 58.1 us; the launch traced here: 57.9 us
  Pallas kernels  56.4 us (97%)
  local copies, waits for them, and re-layouts  1.47 us (3%)
    pallas_call x1, Pallas kernels, body(): pl.pallas_call(kernel, out_shape=jax.ShapeDtypeStruct((COLS // FAM, ROWS)...  56.4 us
    unnamed x1, local copies, waits for them, and re-layouts  1.47 us

profile of v4, /device:TPU:1, one launch (start us, length us, event | category | flops | bytes accessed | tf_op | source)
XLA Modules:
  0.0 57.9 jit_solution(9247026367384724574)
XLA Ops:
  0.0 56.4 %gather_multiply_scatter.1 = bf16[64,512]{1,0:T(8,128)(2,1)} custom-call(s32[8,8,16]{2,1,0:T(8,128)} %bitcast.3, s32[8,16]{1,0:T(8,128)} %counts_ref.1, s32[16]{0:T(128)} %used_ref.1, bf16[512,512]{1,0:T(8,128)(2,1)} %wave_hbm.1, bf16[1,8,512,1024]{3,2,1,0:T(8,128)(2,1)} %left_hbm.1, bf16[1,512,512]{2,1,0:T(8,128)(2,1)} %right_hbm.1), custom_call_target="tpu_custom_call" | custom-call | flops 4294967296 | bytes 9437184 | tf_op jit(solution)/shard_map/gather_multiply_scatter/pallas_call | solution.py:251
  56.4 1.5 %copy.8 = bf16[512,64]{0,1:T(8,128)(2,1)} copy(bf16[512,64]{0,1:T(8,128)(2,1)} %bitcast.2) | data formatting | bytes 131072

commit v5 on v4

--- a/solution.py
+++ b/solution.py
@@ -108,7 +108,7 @@
         load.start()
 
     barrier = pltpu.get_barrier_semaphore()
-    fam_steps = [(dx, dy) for dy in (0, 2) for dx in range(4) if (dx, dy) != (0, 0)]
+    fam_steps = [(2, 2), (1, 2), (3, 2), (0, 2), (2, 0), (1, 0), (3, 0)]
     greeted = [(1, 0, 0, False), (-1, 0, 0, False)]
     greeted += [(0, 1, 0, False), (0, -1, 0, False), (0, 0, 1, False), (0, 0, -1, False), (0, 0, 0, True)]
     for where in greeted:

time: 58.1 us -> 57.4 us (0.988)
  Pallas kernels: 56.4 us -> 55.7 us
    pallas_call x1, Pallas kernels: 56.4 us -> 55.7 us  [body(): pl.pallas_call(kernel, out_shape=jax.ShapeDtypeStruct((COLS // FAM, ROWS)...]
where the time goes in v5:
time: 57.4 us; the launch traced here: 57.2 us
  Pallas kernels  55.7 us (97%)
  local copies, waits for them, and re-layouts  1.47 us (3%)
    pallas_call x1, Pallas kernels, body(): pl.pallas_call(kernel, out_shape=jax.ShapeDtypeStruct((COLS // FAM, ROWS)...  55.7 us
    unnamed x1, local copies, waits for them, and re-layouts  1.47 us

profile of v5, /device:TPU:1, one launch (start us, length us, event | category | flops | bytes accessed | tf_op | source)
XLA Modules:
  0.0 57.2 jit_solution(7194748179947465302)
XLA Ops:
  0.0 55.7 %gather_multiply_scatter.1 = bf16[64,512]{1,0:T(8,128)(2,1)} custom-call(s32[8,8,16]{2,1,0:T(8,128)} %bitcast.3, s32[8,16]{1,0:T(8,128)} %counts_ref.1, s32[16]{0:T(128)} %used_ref.1, bf16[512,512]{1,0:T(8,128)(2,1)} %wave_hbm.1, bf16[1,8,512,1024]{3,2,1,0:T(8,128)(2,1)} %left_hbm.1, bf16[1,512,512]{2,1,0:T(8,128)(2,1)} %right_hbm.1), custom_call_target="tpu_custom_call" | custom-call | flops 4294967296 | bytes 9437184 | tf_op jit(solution)/shard_map/gather_multiply_scatter/pallas_call | solution.py:251
  55.7 1.5 %copy.8 = bf16[512,64]{0,1:T(8,128)(2,1)} copy(bf16[512,64]{0,1:T(8,128)(2,1)} %bitcast.2) | data formatting | bytes 131072

commit v6 on v5

--- a/solution.py
+++ b/solution.py
@@ -104,15 +104,14 @@
         pltpu.make_async_copy(right_hbm, right, load_sem.at[3]),
         pltpu.make_async_copy(left_hbm.at[0, :, :, mine], left.at[0], load_sem.at[2]),
     ]
-    for load in loads:
-        load.start()
-
     barrier = pltpu.get_barrier_semaphore()
     fam_steps = [(2, 2), (1, 2), (3, 2), (0, 2), (2, 0), (1, 0), (3, 0)]
     greeted = [(1, 0, 0, False), (-1, 0, 0, False)]
     greeted += [(0, 1, 0, False), (0, -1, 0, False), (0, 0, 1, False), (0, 0, -1, False), (0, 0, 0, True)]
     for where in greeted:
         pl.semaphore_signal(barrier, inc=1, device_id=device(*where), device_id_type=MESH)
+    for load in loads:
+        load.start()
 
     def chunk_rows(j):
         return pl.ds(pl.multiple_of(lax.rem(x + j, 4) * CHUNK, CHUNK), CHUNK)

time: 57.4 us -> 57.4 us (level)
  no operation moved by 1% of the time
where the time goes in v6:
time: 57.4 us; the launch traced here: 57.2 us
  Pallas kernels  55.7 us (97%)
  local copies, waits for them, and re-layouts  1.47 us (3%)
    pallas_call x1, Pallas kernels, body(): pl.pallas_call(kernel, out_shape=jax.ShapeDtypeStruct((COLS // FAM, ROWS)...  55.7 us
    unnamed x1, local copies, waits for them, and re-layouts  1.47 us

profile of v6, /device:TPU:1, one launch (start us, length us, event | category | flops | bytes accessed | tf_op | source)
XLA Modules:
  0.0 57.2 jit_solution(3891831441051435479)
XLA Ops:
  0.0 55.7 %gather_multiply_scatter.1 = bf16[64,512]{1,0:T(8,128)(2,1)} custom-call(s32[8,8,16]{2,1,0:T(8,128)} %bitcast.3, s32[8,16]{1,0:T(8,128)} %counts_ref.1, s32[16]{0:T(128)} %used_ref.1, bf16[512,512]{1,0:T(8,128)(2,1)} %wave_hbm.1, bf16[1,8,512,1024]{3,2,1,0:T(8,128)(2,1)} %left_hbm.1, bf16[1,512,512]{2,1,0:T(8,128)(2,1)} %right_hbm.1), custom_call_target="tpu_custom_call" | custom-call | flops 4294967296 | bytes 9437184 | tf_op jit(solution)/shard_map/gather_multiply_scatter/pallas_call | solution.py:250
  55.7 1.5 %copy.8 = bf16[512,64]{0,1:T(8,128)(2,1)} copy(bf16[512,64]{0,1:T(8,128)(2,1)} %bitcast.2) | data formatting | bytes 131072
